TPU v7x, 32 devices: a whole 2x2x4 slice. The times are simulated.
32 devices in a mesh: groups: 2 (over y), rows: 4 (over z), cols: 2 (over x), rhs: 2 (over core).
Axes of the slice: x: 2, y: 2, z: 4, core: 2. Of those that a mesh axis runs over, the one named last changes fastest.
Arguments:
- later_solution: bfloat16 [10240, 1024], P(('groups', 'rows', 'cols'), 'rhs'), parts along dimension 0, may hold values from -6 to 6
- factor_panel: bfloat16 [10240, 4, 2048], P(('groups', 'rows'), None, 'cols'), parts along dimension 0, may hold values from -0.078125 to 0.078125
- coupling: bfloat16 [12, 2048, 2048], P('groups', 'rows', 'cols'), parts along dimension 0, may hold values from -0.125 to 0.125
- inverse_diag: bfloat16 [8, 2048, 2048], P('groups', 'rows', 'cols'), parts along dimension 0, as said below
- right_side: bfloat16 [8, 2048, 1024], P('groups', 'cols', 'rhs'), parts along dimension 0, may hold values from -6 to 6
Outputs:
- window_solution: bfloat16 [8, 2048, 1024], P('groups', ('rows', 'cols'), 'rhs'), parts along dimension 0
There are 2 independent parts, one for each index of `groups`. A program takes and returns all parts, laid end to end along the dimension named above; each array names one. Nothing has to cross between parts.
Inputs may be any that keep to these rules, and one draw needn't show every extreme that they name: Each inverse_diag[k] is upper triangular (zero below its diagonal) with a positive diagonal.
All inputs are finite; a program needn't handle non-finite values.
Results may differ from a plain program's by a relative error of at most 0.0073.
Values may be sent and summed in bfloat16 or wider, within the bound.
A program may use at most 128 MiB of HBM per device.

v0:
```python
import jax
import jax.numpy as jnp
from jax import lax
from jax.sharding import PartitionSpec as P


def pair_lookup(blocks):
    mapping = {}
    counter = 0
    for current in range(blocks - 2, -1, -1):
        for source in range(current + 1, blocks):
            mapping[source, current] = counter
            counter += 1
    return mapping


def make_column_terms(earlier_block, sources):

    def column_terms(offset, length):
        partial_value = earlier_block
        for solved_rows, factor_tile in sources:
            partial_value = partial_value + lax.dot_general(
                factor_tile,
                solved_rows,
                (((0,), (0,)), ((), ())),
                preferred_element_type=jnp.float32,
            )
        return partial_value

    return column_terms


def on_device(later_solution, factor_panel, coupling, inverse_diag, right_side):
    lat_rows, blocks, block_cols = factor_panel.shape
    rhs_cols = later_solution.shape[1]
    own_rows = inverse_diag.shape[1]
    flattened = factor_panel.reshape(lat_rows, blocks * block_cols)
    earlier = lax.dot_general(
        flattened,
        lax.all_gather(later_solution, "cols", axis=0, tiled=True),
        (((0,), (0,)), ((), ())),
        preferred_element_type=jnp.float32,
    )
    earlier = earlier.reshape(blocks, block_cols, rhs_cols)
    lookup = pair_lookup(blocks)
    solved = {}
    pieces_out = {}
    piece_rows = own_rows // lax.axis_size("cols")
    for current in range(blocks - 1, -1, -1):
        sources = [
            (solved[source], coupling[lookup[source, current]])
            for source in range(current + 1, blocks)
        ]
        column_terms = make_column_terms(earlier[current], sources)
        summed = lax.psum(column_terms(0, block_cols), "rows")
        residual = (right_side[current].astype(jnp.float32) - summed).astype(jnp.bfloat16)
        diag_block = inverse_diag[current]
        totals = lax.psum(jnp.dot(diag_block, residual, preferred_element_type=jnp.float32), "cols")
        finished = totals.astype(jnp.bfloat16)
        solved[current] = finished
        pieces_out[current] = lax.dynamic_slice_in_dim(
            finished, lax.axis_index("cols") * piece_rows, piece_rows, 0
        )
    return jnp.stack([pieces_out[current] for current in range(blocks)])


def solution(mesh):
    placed = (
        P(("groups", "rows", "cols"), "rhs"),
        P(("groups", "rows"), None, "cols"),
        P("groups", "rows", "cols"),
        P("groups", "rows", "cols"),
        P("groups", "cols", "rhs"),
    )
    return jax.shard_map(
        on_device,
        mesh=mesh,
        in_specs=placed,
        out_specs=P("groups", ("rows", "cols"), "rhs"),
        check_vma=False,
    )
```

profile of v0, /device:TPU:0, one launch (start us, length us, event | category | flops | bytes accessed | tf_op | source)
XLA Modules:
  0.0 546.1 jit_solution(4714201874523483755)
XLA Ops:
  6.5 0.7 all-gather.2.cloned.1.call-update
  7.3 14.9 %copy.10 = bf16[160,8,4,1024]{3,1,2,0:T(8,128)(2,1)} copy(bf16[160,8,4,1024]{3,2,1,0:T(4,128)(2,1)} %bitcast.88) | data formatting | bytes 20971520
  22.2 13.7 %all-gather.2.cloned.1.call-done = bf16[1280,512]{1,0:T(8,128)(2,1)} async-done(((bf16[640,512]{1,0:T(8,128)(2,1)}), bf16[1280,512]{1,0:T(8,128)(2,1)}) %all-gather.2.cloned.1.call-update) | async-done | bytes 1310736 | tf_op jit(solution)/shard_map/all_gather | solution.py:40
  35.9 9.0 %fusion.42 = f32[4096,512]{1,0:T(8,128)S(1)} fusion(bf16[1280,4096]{1,0:T(8,128)(2,1)} %bitcast.89, bf16[1280,512]{1,0:T(8,128)(2,1)} %all-gather.2.cloned.1.call-done), kind=kOutput, calls=%fused_computation.54 | convolution fusion | flops 5368709120 | bytes 20185088 | tf_op jit(solution)/shard_map/dot_general | solution.py:38
  44.9 3.2 copy-done
  48.1 1.5 slice.79
  49.6 0.0 all-reduce.11.cloned.1.call-start
  49.7 86.6 %all-reduce.9.cloned.1.call-done = f32[1024,512]{1,0:T(8,128)} async-done(((f32[1024,512]{1,0:T(8,128)}), f32[1024,512]{1,0:T(8,128)}) %all-reduce.9.cloned.1.call-update) | async-done | bytes 2097168 | tf_op jit(solution)/shard_map/psum | solution.py:55
  136.3 3.0 convolution_bitcast_fusion.3
  139.3 29.2 %all-reduce.16 = bf16[512,512]{0,1:T(8,128)(2,1)S(1)} all-reduce(f32[512,512]{0,1:T(8,128)S(1)} %convolution_bitcast_fusion.3), channel_id=1, replica_groups=mesh['groups'=2,'rows'=4,'cols'=2,'rhs'=2] {'cols'}, use_global_device_ids=true, to_apply=%region_1.0 | all-reduce | flops 262144 | bytes 1572864 | tf_op jit(solution)/shard_map/psum | solution.py:58
  168.5 4.0 slice_add_fusion
  172.5 0.0 all-reduce.13.cloned.1.call-start
  172.5 85.1 %all-reduce.11.cloned.1.call-done = f32[1024,512]{1,0:T(8,128)} async-done(((f32[1024,512]{1,0:T(8,128)}), f32[1024,512]{1,0:T(8,128)}) %all-reduce.11.cloned.1.call-update) | async-done | bytes 2097168 | tf_op jit(solution)/shard_map/psum | solution.py:55
  257.7 2.9 convolution_bitcast_fusion.2
  260.6 29.0 %all-reduce.17 = bf16[512,512]{0,1:T(8,128)(2,1)S(1)} all-reduce(f32[512,512]{0,1:T(8,128)S(1)} %convolution_bitcast_fusion.2), channel_id=1, replica_groups=mesh['groups'=2,'rows'=4,'cols'=2,'rhs'=2] {'cols'}, use_global_device_ids=true, to_apply=%region_3.0 | all-reduce | flops 262144 | bytes 1572864 | tf_op jit(solution)/shard_map/psum | solution.py:58
  289.6 2.0 fusion.23
  291.6 4.0 fusion
  295.7 2.0 fusion.17
  297.7 83.1 %all-reduce.13.cloned.1.call-done = f32[1024,512]{1,0:T(8,128)} async-done(((f32[1024,512]{1,0:T(8,128)}), f32[1024,512]{1,0:T(8,128)}) %all-reduce.13.cloned.1.call-update) | async-done | bytes 2097168 | tf_op jit(solution)/shard_map/psum | solution.py:55
  380.8 3.9 convolution_bitcast_fusion.1
  384.8 30.0 %all-reduce.18 = bf16[512,512]{0,1:T(8,128)(2,1)} all-reduce(f32[512,512]{0,1:T(8,128)} %convolution_bitcast_fusion.1), channel_id=1, replica_groups=mesh['groups'=2,'rows'=4,'cols'=2,'rhs'=2] {'cols'}, use_global_device_ids=true, to_apply=%region_5.0 | all-reduce | flops 262144 | bytes 1572864 | tf_op jit(solution)/shard_map/psum | solution.py:58
  414.8 2.1 fusion.19
  416.9 4.2 fusion.2
  421.2 0.1 copy.9
  421.3 0.1 copy.8
  421.5 0.6 copy-done.1
  422.2 0.1 copy.7
  422.3 84.0 %all-reduce.15.cloned.1.call-done = f32[1024,512]{1,0:T(8,128)} async-done(((f32[1024,512]{1,0:T(8,128)}), f32[1024,512]{1,0:T(8,128)}) %all-reduce.15.cloned.1.call-update) | async-done | bytes 2097168 | tf_op jit(solution)/shard_map/psum | solution.py:55
  506.3 2.9 convolution_bitcast_fusion
  509.3 29.0 %all-reduce.19 = bf16[512,512]{0,1:T(8,128)(2,1)S(1)} all-reduce(f32[512,512]{0,1:T(8,128)S(1)} %convolution_bitcast_fusion), channel_id=1, replica_groups=mesh['groups'=2,'rows'=4,'cols'=2,'rhs'=2] {'cols'}, use_global_device_ids=true, to_apply=%region_7.0 | all-reduce | flops 262144 | bytes 1572864 | tf_op jit(solution)/shard_map/psum | solution.py:58
  538.3 0.1 copy.6
  538.5 1.1 pad_maximum_fusion
  (13 shorter events, 0.2 us)
Async XLA Ops:
  6.5 29.3 %all-gather.2.cloned.1.call-start = ((), (), s32[]{:S(2)}) async-start(), calls=%async_computation | async-start | bytes 1966080 | tf_op jit(solution)/shard_map/all_gather | solution.py:40
  7.3 129.0 %all-reduce.9.cloned.1.call-start = ((), (), s32[]{:S(2)}) async-start(), calls=%async_computation.1 | async-start | bytes 4194304 | tf_op jit(solution)/shard_map/psum | solution.py:55
  44.9 3.2 copy-start
  49.6 208.1 %all-reduce.11.cloned.1.call-start = ((), (), s32[]{:S(2)}) async-start(), calls=%async_computation.2 | async-start | bytes 4194304 | tf_op jit(solution)/shard_map/psum | solution.py:55
  172.5 208.4 %all-reduce.13.cloned.1.call-start = ((), (), s32[]{:S(2)}) async-start(), calls=%async_computation.3 | async-start | bytes 4194304 | tf_op jit(solution)/shard_map/psum | solution.py:55
  295.7 210.7 %all-reduce.15.cloned.1.call-start = ((), (), s32[]{:S(2)}) async-start(), calls=%async_computation.4 | async-start | bytes 4194304 | tf_op jit(solution)/shard_map/psum | solution.py:55
  421.1 1.0 copy-start.1
Sparse Core Ops, SparseCore 0:
  8.9 26.9 all-gather.1
  49.7 86.4 all-reduce.8
  172.6 85.0 all-reduce.10
  295.8 85.0 all-reduce.12
  421.2 85.0 all-reduce.14
where the time goes:
time: 547 us; the launch traced here: 546 us
  waiting for transfers between devices  353 us (65%)
  blocking collectives  117 us (21%)
  matrix products  40.1 us (7%)
  local copies, waits for them, and re-layouts  20.9 us (4%)
  between operations  13.3 us (2%)
    psum x4, waiting for transfers between devices, on_device(): summed = lax.psum(column_terms(0, block_cols), 'rows')  339 us
    psum x4, blocking collectives, on_device(): lax.psum(jnp.dot(diag_block, residual, preferred_element_type=jnp.float32...  117 us
    unnamed x5, local copies, waits for them, and re-layouts  18.8 us
    dot_general x6, matrix products, column_terms(): lax.dot_general(factor_tile, solved_rows, (((0,), (0,)), ((), ())), prefe...  18.3 us
    all_gather x1, waiting for transfers between devices, on_device(): lax.all_gather(later_solution, 'cols', axis=0, tiled=True)  13.7 us
    dot_general x4, matrix products, on_device(): jnp.dot(diag_block, residual, preferred_element_type=jnp.float32)  12.8 us
  transfers between devices with their start and end apart: 5, of which 5 were waited for; matrix products, arithmetic and copies ran while one was open for 3% of the time, Pallas kernels for 0%

commit v1 on v0

v1 whole, which is shorter than its diff:
```python
import functools

import jax
import jax.numpy as jnp
from jax import lax
from jax.experimental import pallas as pl
from jax.experimental.pallas import tpu as pltpu
from jax.sharding import PartitionSpec as P

F32, BF16 = jnp.float32, jnp.bfloat16
MESH = pl.DeviceIdType.MESH
CHUNKS = 4
HOP_LAG = 2
SWAP_LAG = 4
LEAD = 2


def nn(a, b):
    return lax.dot_general(a, b, (((1,), (0,)), ((), ())), preferred_element_type=F32)


def nt(a, b):
    return lax.dot_general(a, b, (((1,), (1,)), ((), ())), preferred_element_type=F32)


def transposed(a):
    return a.astype(F32).T


def kernel(
    nz, nx, chunks, subs,
    later, panel, coup, inv, rhs, out,
    panel_v, coup_v, inv_v, rhs_v, later_v, later_t, acc, from_lo, from_hi, to_hi, to_lo,
    prod, swap_out, swap_in, sol, out_v,
    panel_s, coup_s, inv_s, rhs_s, later_s, out_s,
    gather_ss, gather_rs, hi_ss, lo_ss, lo_rs, hi_rs, swap_ss, swap_rs,
):
    z = lax.axis_index("rows")
    x = lax.axis_index("cols")
    blocks, depth, bc = panel_v.shape
    pairs, _, own, qc = coup_v.shape
    cw = rhs_v.shape[3]
    lr = depth // nx
    piece = own // nx
    last_z = nz - 1
    far = jnp.maximum(z, last_z - z)
    period = max(chunks * subs, subs - 1 + HOP_LAG * last_z + SWAP_LAG)

    barrier = pltpu.get_barrier_semaphore()

    @pl.when(z > 0)
    def _():
        pl.semaphore_signal(barrier, inc=1, device_id={"rows": z - 1}, device_id_type=MESH)

    @pl.when(z < last_z)
    def _():
        pl.semaphore_signal(barrier, inc=1, device_id={"rows": z + 1}, device_id_type=MESH)

    def peer(d):
        return lax.rem(x + d, nx)

    def source(d):
        return lax.rem(x + nx - d, nx)

    for d in range(1, nx):
        pl.semaphore_signal(barrier, inc=1, device_id={"cols": peer(d)}, device_id_type=MESH)

    def load_later(c):
        return pltpu.make_async_copy(
            later.at[:, pl.ds(c * cw, cw)], later_v.at[c, pl.ds(pl.multiple_of(x * lr, 16), lr), :], later_s.at[c])

    def load_panel(i):
        return pltpu.make_async_copy(panel.at[blocks - 1 - i], panel_v.at[i], panel_s.at[i])

    def load_inv(i, q):
        return pltpu.make_async_copy(
            inv.at[blocks - 1 - i, :, pl.ds(q * qc, qc)], inv_v.at[i, q], inv_s.at[i, q])

    def load_rhs(i, c):
        return pltpu.make_async_copy(
            rhs.at[blocks - 1 - i, :, pl.ds(c * cw, cw)], rhs_v.at[i, c], rhs_s.at[i, c])

    def load_coup(p, q):
        return pltpu.make_async_copy(
            coup.at[p, :, pl.ds(q * qc, qc)], coup_v.at[p, q], coup_s.at[p, q])

    for c in range(chunks):
        load_later(c).start()
    load_panel(0).start()

    greeted = (nx - 1) + jnp.where(z > 0, 1, 0) + jnp.where(z < last_z, 1, 0)
    pl.semaphore_wait(barrier, greeted)

    def gather(c, d, who, place):
        return pltpu.make_async_remote_copy(
            src_ref=later.at[:, pl.ds(c * cw, cw)],
            dst_ref=later_v.at[c, pl.ds(pl.multiple_of(place * lr, 16), lr), :],
            send_sem=gather_ss.at[c, d - 1], recv_sem=gather_rs.at[c, d - 1],
            device_id={"cols": who}, device_id_type=MESH)

    for c in range(chunks):
        for d in range(1, nx):
            gather(c, d, peer(d), x).start()

    for i in range(blocks):
        if i > 0:
            load_panel(i).start()
        for q in range(subs):
            load_inv(i, q).start()
        for c in range(chunks):
            load_rhs(i, c).start()
    for p in range(pairs):
        for q in range(subs):
            load_coup(p, q).start()

    @pl.when(z == 0)
    def _():
        @pl.loop(0, blocks * chunks * subs)
        def _(i):
            from_lo[i] = jnp.zeros((cw, qc), BF16)

    @pl.when(z == last_z)
    def _():
        @pl.loop(0, blocks * chunks * subs)
        def _(i):
            from_hi[i] = jnp.zeros((cw, qc), BF16)

    def send_hi(slot, idx):
        return pltpu.make_async_remote_copy(
            src_ref=to_hi.at[slot], dst_ref=from_lo.at[idx],
            send_sem=hi_ss.at[slot], recv_sem=lo_rs.at[idx],
            device_id={"rows": jnp.minimum(z + 1, last_z)}, device_id_type=MESH)

    def send_lo(slot, idx):
        return pltpu.make_async_remote_copy(
            src_ref=to_lo.at[slot], dst_ref=from_hi.at[idx],
            send_sem=lo_ss.at[slot], recv_sem=hi_rs.at[idx],
            device_id={"rows": jnp.maximum(z - 1, 0)}, device_id_type=MESH)

    def swap(i, c, d):
        return pltpu.make_async_remote_copy(
            src_ref=swap_out.at[i, c], dst_ref=swap_in.at[i, c, d - 1],
            send_sem=swap_ss.at[i, c, d - 1], recv_sem=swap_rs.at[i, c, d - 1],
            device_id={"cols": peer(d)}, device_id_type=MESH)

    def store_out(i, c):
        return pltpu.make_async_copy(
            out_v.at[i, c, pl.ds(pl.multiple_of(x * piece, 16), piece), :],
            out.at[blocks - 1 - i, :, pl.ds(pl.multiple_of(c * cw, cw), cw)],
            out_s.at[i, c])

    def decode(tau):
        at = jnp.maximum(tau, 0)
        i = lax.div(at, period)
        r = at - i * period
        valid = (tau >= 0) & (i < blocks) & (r < chunks * subs)
        return valid, i, lax.div(r, subs), lax.rem(r, subs)

    def finish_block(t):
        valid, i, c, q = decode(t - HOP_LAG * far - SWAP_LAG)

        @pl.when(valid & (q == subs - 1))
        def _():
            total = prod[c]
            for d in range(1, nx):
                swap(i, c, d).wait()
                total = total + swap_in[i, c, d - 1].astype(F32)
            sol[c] = total.astype(BF16)

            @pl.loop(i + 1, blocks)
            def _(target):
                p = lax.div(target * (target - 1), 2) + target - 1 - i

                @pl.when(c == 0)
                def _():
                    for s in range(subs):
                        load_coup(p, s).wait()

                for s in range(subs):
                    acc[target, c, s] += nn(sol[c], coup_v[p, s])

            out_v[i, c] = transposed(sol[c]).astype(BF16)
            store_out(i, c).start()

    def flow_hi(t):
        valid, i, c, q = decode(t - HOP_LAG * z)

        @pl.when(valid & (z < last_z))
        def _():
            slot = c * subs + q
            idx = i * (chunks * subs) + slot

            @pl.when(z > 0)
            def _():
                send_hi(slot, idx).wait_recv()

            @pl.when(i > 0)
            def _():
                send_hi(slot, idx).wait_send()

            to_hi[slot] = (acc[i, c, q] + from_lo[idx].astype(F32)).astype(BF16)
            send_hi(slot, idx).start()

    def flow_lo(t):
        valid, i, c, q = decode(t - HOP_LAG * (last_z - z))

        @pl.when(valid & (z > 0))
        def _():
            slot = c * subs + q
            idx = i * (chunks * subs) + slot

            @pl.when(z < last_z)
            def _():
                send_lo(slot, idx).wait_recv()

            @pl.when(i > 0)
            def _():
                send_lo(slot, idx).wait_send()

            to_lo[slot] = (acc[i, c, q] + from_hi[idx].astype(F32)).astype(BF16)
            send_lo(slot, idx).start()

    def diagonal(t):
        valid, i, c, q = decode(t - HOP_LAG * far)

        @pl.when(valid)
        def _():
            slot = c * subs + q
            idx = i * (chunks * subs) + slot

            @pl.when((c == 0) & (q == 0))
            def _():
                for s in range(subs):
                    load_inv(i, s).wait()
                for s in range(chunks):
                    load_rhs(i, s).wait()

            right = transposed(rhs_v[i, c, pl.ds(pl.multiple_of(q * qc, qc), qc), :])

            if nz > 1:
                @pl.when(z == last_z)
                def _():
                    send_hi(slot, idx).wait_recv()

                @pl.when(z == 0)
                def _():
                    send_lo(slot, idx).wait_recv()

            total = acc[i, c, q] + from_lo[idx].astype(F32) + from_hi[idx].astype(F32)
            residual = (right - total).astype(BF16)
            term = nt(residual, inv_v[i, q])

            @pl.when(q == 0)
            def _():
                prod[c] = term

            @pl.when(q > 0)
            def _():
                prod[c] += term

            @pl.when(q == subs - 1)
            def _():
                swap_out[i, c] = prod[c].astype(BF16)
                for d in range(1, nx):
                    swap(i, c, d).start()

    def later_terms(t):
        u = t + LEAD
        c = lax.div(u, subs)
        for j in range(-(-blocks // subs)):
            i = lax.rem(u, subs) + j * subs

            @pl.when((c < chunks) & (i < blocks))
            def _():
                @pl.when(i == 0)
                def _():
                    load_later(c).wait()
                    for d in range(1, nx):
                        gather(c, d, peer(d), source(d)).wait_recv()
                    later_t[c] = transposed(later_v[c]).astype(BF16)

                @pl.when(c == 0)
                def _():
                    load_panel(i).wait()

                for s in range(subs):
                    acc[i, c, s] = nn(later_t[c], panel_v[i, :, s * qc:(s + 1) * qc])

    steps = LEAD + (blocks - 1) * period + chunks * subs + HOP_LAG * last_z + SWAP_LAG

    def tick(u, carry):
        t = u - LEAD
        finish_block(t)
        flow_hi(t)
        flow_lo(t)
        diagonal(t)
        later_terms(t)
        return carry

    lax.fori_loop(0, steps, tick, 0)

    for c in range(chunks):
        for d in range(1, nx):
            gather(c, d, peer(d), x).wait_send()

    @pl.when(z < last_z)
    def _():
        @pl.loop(0, chunks * subs)
        def _(slot):
            send_hi(slot, slot).wait_send()

    @pl.when(z > 0)
    def _():
        @pl.loop(0, chunks * subs)
        def _(slot):
            send_lo(slot, slot).wait_send()

    for i in range(blocks):
        for c in range(chunks):
            store_out(i, c).wait()


def on_device(nz, nx, later_solution, factor_panel, coupling, inverse_diag, right_side):
    depth, blocks, bc = factor_panel.shape
    rhs_cols = later_solution.shape[1]
    pairs, own, _ = coupling.shape
    subs = max(1, min(4, bc // 128))
    chunks = CHUNKS
    cw, qc = rhs_cols // chunks, bc // subs
    per_block = chunks * subs
    others = max(nx - 1, 1)
    panel = jnp.transpose(factor_panel, (1, 0, 2))
    dma = pltpu.SemaphoreType.DMA
    vmem = pltpu.VMEM
    flops = 2 * rhs_cols * bc * (depth * blocks + own * (pairs + blocks))
    return pl.pallas_call(
        functools.partial(kernel, nz, nx, chunks, subs),
        out_shape=jax.ShapeDtypeStruct((blocks, own // nx, rhs_cols), BF16),
        in_specs=[pl.BlockSpec(memory_space=pl.ANY)] * 5,
        out_specs=pl.BlockSpec(memory_space=pl.ANY),
        scratch_shapes=[
            vmem((blocks, depth, bc), BF16),
            vmem((pairs, subs, own, qc), BF16),
            vmem((blocks, subs, own, qc), BF16),
            vmem((blocks, chunks, bc, cw), BF16),
            vmem((chunks, depth, cw), BF16),
            vmem((chunks, cw, depth), BF16),
            vmem((blocks, chunks, subs, cw, qc), F32),
            vmem((blocks * per_block, cw, qc), BF16),
            vmem((blocks * per_block, cw, qc), BF16),
            vmem((per_block, cw, qc), BF16),
            vmem((per_block, cw, qc), BF16),
            vmem((chunks, cw, own), F32),
            vmem((blocks, chunks, cw, own), BF16),
            vmem((blocks, chunks, others, cw, own), BF16),
            vmem((chunks, cw, own), BF16),
            vmem((blocks, chunks, own, cw), BF16),
            dma((blocks,)), dma((pairs, subs)), dma((blocks, subs)), dma((blocks, chunks)),
            dma((chunks,)), dma((blocks, chunks)),
            dma((chunks, others)), dma((chunks, others)),
            dma((per_block,)), dma((per_block,)),
            dma((blocks * per_block,)), dma((blocks * per_block,)),
            dma((blocks, chunks, others)), dma((blocks, chunks, others)),
        ],
        compiler_params=pltpu.CompilerParams(
            collective_id=0, has_side_effects=True, vmem_limit_bytes=60 * 2**20),
        cost_estimate=pl.CostEstimate(
            flops=flops, bytes_accessed=2 * (depth * blocks * bc + own * bc * (pairs + blocks)), transcendentals=0),
    )(later_solution, panel, coupling, inverse_diag, right_side)


def solution(mesh):
    placed = (
        P(("groups", "rows", "cols"), "rhs"),
        P(("groups", "rows"), None, "cols"),
        P("groups", "rows", "cols"),
        P("groups", "rows", "cols"),
        P("groups", "cols", "rhs"),
    )
    return jax.shard_map(
        functools.partial(on_device, mesh.shape["rows"], mesh.shape["cols"]),
        mesh=mesh,
        in_specs=placed,
        out_specs=P("groups", ("rows", "cols"), "rhs"),
        check_vma=False,
    )
```

time: 547 us -> 152 us (0.28)
  waiting for transfers between devices: 353 us -> 0 us
  Pallas kernels: 0 us -> 137 us
  blocking collectives: 117 us -> 0 us
  matrix products: 40.1 us -> 0 us
  between operations: 13.3 us -> 0.01 us
  local copies, waits for them, and re-layouts: 20.9 us -> 13.9 us
    psum x4 -> x0, waiting for transfers between devices: 339 us -> none  [on_device(): summed = lax.psum(column_terms(0, block_cols), 'rows')]
    pallas_call x0 -> x1, Pallas kernels: none -> 137 us  [on_device(): pl.pallas_call(functools.partial(kernel, nz, nx, chunks, subs), out_shape...]
    psum x4 -> x0, blocking collectives: 117 us -> none  [on_device(): lax.psum(jnp.dot(diag_block, residual, preferred_element_type=jnp.float32...]
    dot_general x11 -> x0, matrix products: 40.1 us -> none  [the longest x6 18.3 us: column_terms(): lax.dot_general(factor_tile, solved_rows, (((0,), (0,)), ((), ())), prefe...]
    all_gather x1 -> x0, waiting for transfers between devices: 13.7 us -> none  [on_device(): lax.all_gather(later_solution, 'cols', axis=0, tiled=True)]
    unnamed x5 -> x2, local copies, waits for them, and re-layouts: 18.8 us -> 13.9 us
  transfers between devices with their start and end apart: 5 -> 0, of which waited for: 5 -> 0; matrix products, arithmetic and copies ran while one was open for 3% -> 0% of each run, Pallas kernels for 0% -> 0%
where the time goes in v1:
time: 152 us; the launch traced here: 151 us
  Pallas kernels  137 us (90%)
  local copies, waits for them, and re-layouts  13.9 us (9%)
    pallas_call x1, Pallas kernels, on_device(): pl.pallas_call(functools.partial(kernel, nz, nx, chunks, subs), out_shape...  137 us
    unnamed x2, local copies, waits for them, and re-layouts  13.9 us

profile of v1, /device:TPU:0, one launch (start us, length us, event | category | flops | bytes accessed | tf_op | source)
XLA Modules:
  0.0 151.2 jit_solution(4386236775740723272)
XLA Ops:
  0.0 11.6 %copy.8 = bf16[1280,4,1024]{2,0,1:T(8,128)(2,1)} copy(bf16[1280,4,1024]{2,1,0:T(4,128)(2,1)} %param.6) | data formatting | bytes 20971520 | tf_op args[1]
  11.6 137.3 %shard_map.55 = bf16[4,256,512]{2,1,0:T(8,128)(2,1)} custom-call(bf16[640,512]{1,0:T(8,128)(2,1)} %later.1, bf16[4,1280,1024]{2,1,0:T(8,128)(2,1)} %bitcast.3, bf16[6,512,1024]{2,1,0:T(8,128)(2,1)} %coup.1, bf16[4,512,1024]{2,1,0:T(8,128)(2,1)} %inv.1, bf16[4,1024,512]{2,1,0:T(8,128)(2,1)} %rhs.1), custom_call_target="tpu_custom_call" | custom-call | flops 10737418240 | bytes 20971520 | tf_op jit(solution)/shard_map/pallas_call | solution.py:336
  148.9 2.3 %copy.10 = bf16[4,256,512]{2,1,0:T(8,128)(2,1)} copy(bf16[4,256,512]{2,1,0:T(8,128)(2,1)} %shard_map.55) | data formatting | bytes 2097152

commit v2 on v1

--- a/solution.py
+++ b/solution.py
@@ -10,9 +10,10 @@
 F32, BF16 = jnp.float32, jnp.bfloat16
 MESH = pl.DeviceIdType.MESH
 CHUNKS = 4
-HOP_LAG = 2
-SWAP_LAG = 4
-LEAD = 2
+SUBS = 4
+HOP_LAG = 3
+SWAP_LAG = 5
+LEAD = 1
 
 
 def nn(a, b):
@@ -167,20 +168,34 @@
                 total = total + swap_in[i, c, d - 1].astype(F32)
             sol[c] = total.astype(BF16)
 
-            @pl.loop(i + 1, blocks)
-            def _(target):
-                p = lax.div(target * (target - 1), 2) + target - 1 - i
-
-                @pl.when(c == 0)
+            @pl.when(i + 1 < blocks)
+            def _():
+                couple(i, c, i + 1)
+
+    def couple(i, c, target):
+        p = lax.div(target * (target - 1), 2) + target - 1 - i
+
+        @pl.when(c == 0)
+        def _():
+            for s in range(subs):
+                load_coup(p, s).wait()
+
+        for s in range(subs):
+            acc[target, c, s] += nn(sol[c], coup_v[p, s])
+
+    def rest_of_block(t):
+        for delta in range(1, blocks - 1):
+            valid, i, c, q = decode(t - HOP_LAG * far - SWAP_LAG - delta)
+
+            @pl.when(valid & (q == subs - 1))
+            def _():
+                if delta == 1:
+                    out_v[i, c] = transposed(sol[c]).astype(BF16)
+                    store_out(i, c).start()
+
+                @pl.when(i + 1 + delta < blocks)
                 def _():
-                    for s in range(subs):
-                        load_coup(p, s).wait()
-
-                for s in range(subs):
-                    acc[target, c, s] += nn(sol[c], coup_v[p, s])
-
-            out_v[i, c] = transposed(sol[c]).astype(BF16)
-            store_out(i, c).start()
+                    couple(i, c, i + 1 + delta)
 
     def flow_hi(t):
         valid, i, c, q = decode(t - HOP_LAG * z)
@@ -286,7 +301,7 @@
                 for s in range(subs):
                     acc[i, c, s] = nn(later_t[c], panel_v[i, :, s * qc:(s + 1) * qc])
 
-    steps = LEAD + (blocks - 1) * period + chunks * subs + HOP_LAG * last_z + SWAP_LAG
+    steps = LEAD + (blocks - 1) * period + chunks * subs + HOP_LAG * last_z + SWAP_LAG + 1
 
     def tick(u, carry):
         t = u - LEAD
@@ -294,6 +309,7 @@
         flow_hi(t)
         flow_lo(t)
         diagonal(t)
+        rest_of_block(t)
         later_terms(t)
         return carry
 
@@ -324,7 +340,7 @@
     depth, blocks, bc = factor_panel.shape
     rhs_cols = later_solution.shape[1]
     pairs, own, _ = coupling.shape
-    subs = max(1, min(4, bc // 128))
+    subs = max(1, min(SUBS, bc // 128))
     chunks = CHUNKS
     cw, qc = rhs_cols // chunks, bc // subs
     per_block = chunks * subs

time: 152 us -> 131 us (0.86)
  Pallas kernels: 137 us -> 117 us
    pallas_call x1, Pallas kernels: 137 us -> 117 us  [on_device(): pl.pallas_call(functools.partial(kernel, nz, nx, chunks, subs), out_shape...]
where the time goes in v2:
time: 131 us
  Pallas kernels  117 us (89%)
  local copies, waits for them, and re-layouts  13.9 us (11%)
    pallas_call x1, Pallas kernels, on_device(): pl.pallas_call(functools.partial(kernel, nz, nx, chunks, subs), out_shape...  117 us
    unnamed x2, local copies, waits for them, and re-layouts  13.9 us

profile of v2, /device:TPU:0, one launch (start us, length us, event | category | flops | bytes accessed | tf_op | source)
XLA Modules:
  0.0 131.2 jit_solution(11366260598749924957)
XLA Ops:
  0.0 11.6 %copy.8 = bf16[1280,4,1024]{2,0,1:T(8,128)(2,1)} copy(bf16[1280,4,1024]{2,1,0:T(4,128)(2,1)} %param.6) | data formatting | bytes 20971520 | tf_op args[1]
  11.6 117.3 %shard_map.55 = bf16[4,256,512]{2,1,0:T(8,128)(2,1)} custom-call(bf16[640,512]{1,0:T(8,128)(2,1)} %later.1, bf16[4,1280,1024]{2,1,0:T(8,128)(2,1)} %bitcast.3, bf16[6,512,1024]{2,1,0:T(8,128)(2,1)} %coup.1, bf16[4,512,1024]{2,1,0:T(8,128)(2,1)} %inv.1, bf16[4,1024,512]{2,1,0:T(8,128)(2,1)} %rhs.1), custom_call_target="tpu_custom_call" | custom-call | flops 10737418240 | bytes 20971520 | tf_op jit(solution)/shard_map/pallas_call | solution.py:352
  128.9 2.3 %copy.10 = bf16[4,256,512]{2,1,0:T(8,128)(2,1)} copy(bf16[4,256,512]{2,1,0:T(8,128)(2,1)} %shard_map.55) | data formatting | bytes 2097152

commit v3 on v2

--- a/solution.py
+++ b/solution.py
@@ -47,6 +47,9 @@
     far = jnp.maximum(z, last_z - z)
     period = max(chunks * subs, subs - 1 + HOP_LAG * last_z + SWAP_LAG)
 
+    def used(row, col, q):
+        return col * bc + (q + 1) * qc > row * own
+
     barrier = pltpu.get_barrier_semaphore()
 
     @pl.when(z > 0)
@@ -162,11 +165,17 @@
 
         @pl.when(valid & (q == subs - 1))
         def _():
-            total = prod[c]
             for d in range(1, nx):
-                swap(i, c, d).wait()
-                total = total + swap_in[i, c, d - 1].astype(F32)
-            sol[c] = total.astype(BF16)
+                @pl.when(used(z, x, subs - 1))
+                def _():
+                    swap(i, c, d).wait_send()
+
+                @pl.when(used(z, source(d), subs - 1))
+                def _():
+                    swap(i, c, d).wait_recv()
+                    prod[c] += swap_in[i, c, d - 1].astype(F32)
+
+            sol[c] = prod[c].astype(BF16)
 
             @pl.when(i + 1 < blocks)
             def _():
@@ -200,7 +209,7 @@
     def flow_hi(t):
         valid, i, c, q = decode(t - HOP_LAG * z)
 
-        @pl.when(valid & (z < last_z))
+        @pl.when(valid & (z < last_z) & used(z + 1, x, q))
         def _():
             slot = c * subs + q
             idx = i * (chunks * subs) + slot
@@ -238,22 +247,26 @@
     def diagonal(t):
         valid, i, c, q = decode(t - HOP_LAG * far)
 
-        @pl.when(valid)
-        def _():
-            slot = c * subs + q
-            idx = i * (chunks * subs) + slot
-
-            @pl.when((c == 0) & (q == 0))
+        @pl.when(valid & (q == 0))
+        def _():
+            prod[c] = jnp.zeros((cw, own), F32)
+
+            @pl.when(c == 0)
             def _():
                 for s in range(subs):
                     load_inv(i, s).wait()
                 for s in range(chunks):
                     load_rhs(i, s).wait()
 
+        @pl.when(valid & used(z, x, q))
+        def _():
+            slot = c * subs + q
+            idx = i * (chunks * subs) + slot
+
             right = transposed(rhs_v[i, c, pl.ds(pl.multiple_of(q * qc, qc), qc), :])
 
             if nz > 1:
-                @pl.when(z == last_z)
+                @pl.when((z > 0) & ((z == last_z) | jnp.logical_not(used(z + 1, x, q))))
                 def _():
                     send_hi(slot, idx).wait_recv()
 
@@ -265,13 +278,7 @@
             residual = (right - total).astype(BF16)
             term = nt(residual, inv_v[i, q])
 
-            @pl.when(q == 0)
-            def _():
-                prod[c] = term
-
-            @pl.when(q > 0)
-            def _():
-                prod[c] += term
+            prod[c] += term
 
             @pl.when(q == subs - 1)
             def _():
@@ -323,7 +330,9 @@
     def _():
         @pl.loop(0, chunks * subs)
         def _(slot):
-            send_hi(slot, slot).wait_send()
+            @pl.when(used(z + 1, x, lax.rem(slot, subs)))
+            def _():
+                send_hi(slot, slot).wait_send()
 
     @pl.when(z > 0)
     def _():

time: 131 us -> 131 us (level)
  no operation moved by 1% of the time
where the time goes in v3:
time: 131 us
  Pallas kernels  117 us (89%)
  local copies, waits for them, and re-layouts  13.9 us (11%)
    pallas_call x1, Pallas kernels, on_device(): pl.pallas_call(functools.partial(kernel, nz, nx, chunks, subs), out_shape...  117 us
    unnamed x2, local copies, waits for them, and re-layouts  13.9 us

profile of v3, /device:TPU:0, one launch (start us, length us, event | category | flops | bytes accessed | tf_op | source)
XLA Modules:
  0.0 131.2 jit_solution(12738761327420492928)
XLA Ops:
  0.0 11.6 %copy.8 = bf16[1280,4,1024]{2,0,1:T(8,128)(2,1)} copy(bf16[1280,4,1024]{2,1,0:T(4,128)(2,1)} %param.6) | data formatting | bytes 20971520 | tf_op args[1]
  11.6 117.3 %shard_map.55 = bf16[4,256,512]{2,1,0:T(8,128)(2,1)} custom-call(bf16[640,512]{1,0:T(8,128)(2,1)} %later.1, bf16[4,1280,1024]{2,1,0:T(8,128)(2,1)} %bitcast.3, bf16[6,512,1024]{2,1,0:T(8,128)(2,1)} %coup.1, bf16[4,512,1024]{2,1,0:T(8,128)(2,1)} %inv.1, bf16[4,1024,512]{2,1,0:T(8,128)(2,1)} %rhs.1), custom_call_target="tpu_custom_call" | custom-call | flops 10737418240 | bytes 20971520 | tf_op jit(solution)/shard_map/pallas_call | solution.py:361
  128.9 2.3 %copy.10 = bf16[4,256,512]{2,1,0:T(8,128)(2,1)} copy(bf16[4,256,512]{2,1,0:T(8,128)(2,1)} %shard_map.55) | data formatting | bytes 2097152
